TPU v7x, 128 devices: a whole 4x4x4 slice. The times are simulated.
128 devices in a mesh: row: 16 (over z_hi, y, core), col: 8 (over x, z_lo).
Axes of the slice: x: 4, y: 4, z: 4 (z_hi: 2, z_lo: 2; z = z_hi * 2 + z_lo), core: 2. Of those that a mesh axis runs over, the one named last changes fastest.
Arguments:
- trial_vectors: bfloat16 [24576, 256], P(('row', 'col')), may hold values from -6 to 6
- h_blocks: bfloat16 [8, 16, 24, 64, 16, 128], P('col', None, None, None, 'row'), may hold values from -0.09375 to 0.09375
- block_col: int32 [8, 16, 24, 16, 2], P('col', 'row'), may hold values from 0 to 2
- block_count: int32 [8, 16, 24, 16], P('col', 'row'), may hold values from 0 to 2, as said below
- center: float32 [1], replicated, may hold values from -0.5 to 0.5
- half_width: float32 [1], replicated, may hold values from 1.5 to 2.5
Outputs:
- filtered: float32 [24576, 256], P(('row', 'col'))
Inputs may be any that keep to these rules, and one draw needn't show every extreme that they name: Only the first block_count slots of a block row and source domain hold blocks. In every column group one row domain has all 2 slots used in every block row for every source domain.
All inputs are finite; a program needn't handle non-finite values.
Results may differ from a plain program's by a relative error of at most 0.019.
Values may be sent and summed in bfloat16 or wider, within the bound.
A program may use at most 64 MiB of HBM per device.

v0:
```python
import jax
import jax.numpy as jnp
from jax import lax
from jax.sharding import PartitionSpec as P

BLOCK = 64
VECTORS = 256
PER = 2
DEGREE = 6
BLOCK_ROWS = 3


def from_everyone(array, axis):
    copies = jnp.broadcast_to(array, (lax.axis_size(axis), *array.shape))
    return lax.all_to_all(copies, axis, split_axis=0, concat_axis=0, tiled=True)


def in_order(blocks, dim):
    shape = list(blocks.shape[1:])
    shape[dim] *= blocks.shape[0]
    return jnp.moveaxis(blocks, 0, dim).reshape(shape)


def collect(array, axis, dim):
    blocks = from_everyone(array, axis)
    return in_order(blocks, dim)


def cut_along(array, dim, size):
    shape = array.shape
    blocks = array.reshape(*shape[:dim], size, shape[dim] // size, *shape[dim + 1 :])
    return jnp.moveaxis(blocks, dim, 0)


def summed_on_arrival(array, axis, dim):
    blocks = cut_along(array, dim, lax.axis_size(axis))
    arrived = lax.all_to_all(blocks, axis, split_axis=0, concat_axis=0, tiled=True)
    return arrived.astype(jnp.float32).sum(axis=0)


def body(trial_vectors, h_blocks, block_col, block_count, center, half_width):
    arrived = lax.all_to_all(h_blocks, "row", split_axis=1, concat_axis=4, tiled=True)
    row_count = lax.axis_size("row")
    col_count = lax.axis_size("col")
    domain = BLOCK_ROWS * col_count
    filled = (
        lax.broadcasted_iota(jnp.int32, (domain, row_count, PER), 2) < block_count[0, 0][:, :, None]
    )
    shaped = arrived[0, 0].reshape(domain, BLOCK, row_count, PER, BLOCK)
    blocks = jnp.where(filled[:, None, :, :, None], shaped, jnp.zeros((), jnp.bfloat16))
    blocks = blocks.reshape(col_count, BLOCK_ROWS, BLOCK, row_count * PER * BLOCK)
    sources = lax.broadcasted_iota(jnp.int32, (domain, row_count, PER), 1)
    columns = (sources * BLOCK_ROWS + block_col[0, 0]).reshape(
        col_count, BLOCK_ROWS, row_count * PER
    )
    centre_value = center[0]
    half_value = half_width[0]

    def operator(current):
        gathered = collect(current, "row", 0).reshape(row_count * BLOCK_ROWS, BLOCK, VECTORS)

        def group_rows(entries):
            group_blocks, group_columns = entries
            picked = gathered[group_columns].reshape(BLOCK_ROWS, row_count * PER * BLOCK, VECTORS)
            return jnp.einsum(
                "rak,rkv->rav", group_blocks, picked, preferred_element_type=jnp.float32
            )

        partial_value = lax.map(group_rows, (blocks, columns)).reshape(domain * BLOCK, VECTORS)
        owned = summed_on_arrival(partial_value.astype(jnp.bfloat16), "col", 0)
        return owned

    previous = trial_vectors.astype(jnp.float32)
    current = (operator(trial_vectors) - centre_value * previous) / half_value
    for degree_step in range(DEGREE - 1):
        product = operator(current.astype(jnp.bfloat16))
        following = 2.0 * (product - centre_value * current) / half_value - previous
        previous, current = (current, following)
    return current


def solution(mesh):
    in_specs = (
        P(("row", "col"), None),
        P("col", None, None, None, "row", None),
        P("col", "row", None, None, None),
        P("col", "row", None, None),
        P(),
        P(),
    )
    out_specs = P(("row", "col"), None)
    return jax.shard_map(body, mesh=mesh, in_specs=in_specs, out_specs=out_specs, check_vma=False)
```

profile of v0, /device:TPU:1, one launch (start us, length us, event | category | flops | bytes accessed | tf_op | source)
XLA Modules:
  0.0 602.1 jit_solution(9073077212405293290)
XLA Ops:
  0.0 82.7 %all_to_all.75 = bf16[1,16,24,64,1,128]{5,3,4,2,0,1:T(8,128)(2,1)} all-to-all(bf16[1,16,24,64,1,128]{5,3,4,2,0,1:T(8,128)(2,1)} %bitcast.171), channel_id=1, replica_groups=mesh['row'=16,'col'=8] {'row'}, dimensions={1} | all-to-all | bytes 12582912 | tf_op jit(solution)/shard_map/all_to_all | solution.py:42
  90.8 11.1 %copy.27 = bf16[1,1,24,64,16,1,128]{6,4,3,2,5,1,0:T(8,128)(2,1)} copy(bf16[1,1,24,64,16,1,128]{6,3,2,4,5,1,0:T(8,128)(2,1)} %bitcast.170) | data formatting | bytes 12582912 | tf_op jit(solution)/shard_map/all_to_all | solution.py:42
  101.9 10.3 %reshape_squeeze.3 = bf16[8,3,64,2048]{3,2,1,0:T(8,128)(2,1)} reshape(bf16[1,1,24,64,16,1,128]{6,4,3,2,5,1,0:T(8,128)(2,1)} %copy.27) | data formatting | bytes 12582912 | tf_op jit(solution)/shard_map/reshape;squeeze | solution.py:49
  119.2 37.9 %while.60 = (s32[]{:T(128)}, bf16[8,3,64,256]{3,2,1,0:T(8,128)(2,1)}, bf16[8,3,64,2048]{3,2,1,0:T(8,128)(2,1)}, s32[8,3,32]{2,0,1:T(8,128)S(1)}, bf16[48,64,256]{2,1,0:T(8,128)(2,1)}, /*index=5*/s32[]{:T(128)}) while((s32[]{:T(128)}, bf16[8,3,64,256]{3,2,1,0:T(8,128)(2,1)}, bf16[8,3,64,2048]{3,2,1,0:T(8,128)(2,1)}, s32[8,3,32]{2,0,1:T(8,128)S(1)}, ...), condition=%wide.region_1.2_spmd, body=%wide.region_0.1_spmd.sunk | while | flops 201327904 | bytes 10427721 | solution.py:69
  162.8 10.7 %all-to-all-done.2 = bf16[8,192,256]{2,1,0:T(8,128)(2,1)S(1)} async-done(((bf16[8,192,256]{2,1,0:T(8,128)(2,1)}), bf16[8,192,256]{2,1,0:T(8,128)(2,1)S(1)}, u32[]{:S(2)}, u32[]{:S(2)}) %all-to-all-start.2) | async-done | bytes 786464 | tf_op jit(solution)/shard_map/all_to_all | solution.py:37
  175.1 8.9 %all-to-all-start.3 = ((bf16[16,192,256]{2,1,0:T(8,128)(2,1)}), bf16[16,192,256]{2,1,0:T(8,128)(2,1)}, u32[]{:S(2)}, u32[]{:S(2)}) async-start(bf16[16,192,256]{2,1,0:T(8,128)(2,1)} %broadcast_in_dim.65), calls=%async_computation.3 | async-start | bytes 3145728 | tf_op jit(solution)/shard_map/all_to_all | solution.py:15
  184.0 23.1 %all-to-all-done.3 = bf16[16,192,256]{2,1,0:T(8,128)(2,1)} async-done(((bf16[16,192,256]{2,1,0:T(8,128)(2,1)}), bf16[16,192,256]{2,1,0:T(8,128)(2,1)}, u32[]{:S(2)}, u32[]{:S(2)}) %all-to-all-start.3) | async-done | bytes 1572896 | tf_op jit(solution)/shard_map/all_to_all | solution.py:15
  208.1 37.9 %while.61 = (s32[]{:T(128)}, bf16[8,3,64,256]{3,2,1,0:T(8,128)(2,1)}, bf16[8,3,64,2048]{3,2,1,0:T(8,128)(2,1)}, s32[8,3,32]{2,0,1:T(8,128)S(1)}, bf16[48,64,256]{2,1,0:T(8,128)(2,1)}, /*index=5*/s32[]{:T(128)}) while((s32[]{:T(128)}, bf16[8,3,64,256]{3,2,1,0:T(8,128)(2,1)}, bf16[8,3,64,2048]{3,2,1,0:T(8,128)(2,1)}, s32[8,3,32]{2,0,1:T(8,128)S(1)}, ...), condition=%wide.region_4.5_spmd, body=%wide.region_3.4_spmd.sunk | while | flops 201327904 | bytes 10427721 | solution.py:69
  246.0 14.8 %all_to_all.76 = bf16[8,192,256]{2,1,0:T(8,128)(2,1)S(1)} all-to-all(bf16[8,192,256]{2,1,0:T(8,128)(2,1)} %bitcast.174), channel_id=1, replica_groups=mesh['row'=16,'col'=8] {'col'}, dimensions={0} | all-to-all | bytes 1572864 | tf_op jit(solution)/shard_map/all_to_all | solution.py:37
  263.0 6.3 %all-to-all-start.5 = ((bf16[16,192,256]{2,1,0:T(8,128)(2,1)}), bf16[16,192,256]{2,1,0:T(8,128)(2,1)}, u32[]{:S(2)}, u32[]{:S(2)}) async-start(bf16[16,192,256]{2,1,0:T(8,128)(2,1)} %broadcast_in_dim.66), calls=%async_computation.5 | async-start | bytes 3145728 | tf_op jit(solution)/shard_map/all_to_all | solution.py:15
  269.3 23.2 %all-to-all-done.5 = bf16[16,192,256]{2,1,0:T(8,128)(2,1)} async-done(((bf16[16,192,256]{2,1,0:T(8,128)(2,1)}), bf16[16,192,256]{2,1,0:T(8,128)(2,1)}, u32[]{:S(2)}, u32[]{:S(2)}) %all-to-all-start.5) | async-done | bytes 1572896 | tf_op jit(solution)/shard_map/all_to_all | solution.py:15
  293.5 37.9 %while.62 = (s32[]{:T(128)}, bf16[8,3,64,256]{3,2,1,0:T(8,128)(2,1)}, bf16[8,3,64,2048]{3,2,1,0:T(8,128)(2,1)}, s32[8,3,32]{2,0,1:T(8,128)S(1)}, bf16[48,64,256]{2,1,0:T(8,128)(2,1)}, /*index=5*/s32[]{:T(128)}) while((s32[]{:T(128)}, bf16[8,3,64,256]{3,2,1,0:T(8,128)(2,1)}, bf16[8,3,64,2048]{3,2,1,0:T(8,128)(2,1)}, s32[8,3,32]{2,0,1:T(8,128)S(1)}, ...), condition=%wide.region_7.8_spmd, body=%wide.region_6.7_spmd.sunk | while | flops 201327904 | bytes 10427721 | solution.py:69
  331.3 14.8 %all_to_all.77 = bf16[8,192,256]{2,1,0:T(8,128)(2,1)S(1)} all-to-all(bf16[8,192,256]{2,1,0:T(8,128)(2,1)} %bitcast.175), channel_id=1, replica_groups=mesh['row'=16,'col'=8] {'col'}, dimensions={0} | all-to-all | bytes 1572864 | tf_op jit(solution)/shard_map/all_to_all | solution.py:37
  348.7 6.3 %all-to-all-start.7 = ((bf16[16,192,256]{2,1,0:T(8,128)(2,1)}), bf16[16,192,256]{2,1,0:T(8,128)(2,1)}, u32[]{:S(2)}, u32[]{:S(2)}) async-start(bf16[16,192,256]{2,1,0:T(8,128)(2,1)} %broadcast_in_dim.67), calls=%async_computation.7 | async-start | bytes 3145728 | tf_op jit(solution)/shard_map/all_to_all | solution.py:15
  355.0 23.2 %all-to-all-done.7 = bf16[16,192,256]{2,1,0:T(8,128)(2,1)} async-done(((bf16[16,192,256]{2,1,0:T(8,128)(2,1)}), bf16[16,192,256]{2,1,0:T(8,128)(2,1)}, u32[]{:S(2)}, u32[]{:S(2)}) %all-to-all-start.7) | async-done | bytes 1572896 | tf_op jit(solution)/shard_map/all_to_all | solution.py:15
  379.2 37.9 %while.63 = (s32[]{:T(128)}, bf16[8,3,64,256]{3,2,1,0:T(8,128)(2,1)}, bf16[8,3,64,2048]{3,2,1,0:T(8,128)(2,1)}, s32[8,3,32]{2,0,1:T(8,128)S(1)}, bf16[48,64,256]{2,1,0:T(8,128)(2,1)}, /*index=5*/s32[]{:T(128)}) while((s32[]{:T(128)}, bf16[8,3,64,256]{3,2,1,0:T(8,128)(2,1)}, bf16[8,3,64,2048]{3,2,1,0:T(8,128)(2,1)}, ...), condition=%wide.region_10.11_spmd, body=%wide.region_9.10_spmd.sunk | while | flops 201327904 | bytes 10427721 | solution.py:69
  417.0 14.8 %all_to_all.78 = bf16[8,192,256]{2,1,0:T(8,128)(2,1)S(1)} all-to-all(bf16[8,192,256]{2,1,0:T(8,128)(2,1)} %bitcast.176), channel_id=1, replica_groups=mesh['row'=16,'col'=8] {'col'}, dimensions={0} | all-to-all | bytes 1572864 | tf_op jit(solution)/shard_map/all_to_all | solution.py:37
  434.1 6.3 %all-to-all-start.9 = ((bf16[16,192,256]{2,1,0:T(8,128)(2,1)}), bf16[16,192,256]{2,1,0:T(8,128)(2,1)}, u32[]{:S(2)}, u32[]{:S(2)}) async-start(bf16[16,192,256]{2,1,0:T(8,128)(2,1)} %broadcast_in_dim.68), calls=%async_computation.9 | async-start | bytes 3145728 | tf_op jit(solution)/shard_map/all_to_all | solution.py:15
  440.3 23.2 %all-to-all-done.9 = bf16[16,192,256]{2,1,0:T(8,128)(2,1)} async-done(((bf16[16,192,256]{2,1,0:T(8,128)(2,1)}), bf16[16,192,256]{2,1,0:T(8,128)(2,1)}, u32[]{:S(2)}, u32[]{:S(2)}) %all-to-all-start.9) | async-done | bytes 1572896 | tf_op jit(solution)/shard_map/all_to_all | solution.py:15
  464.5 37.9 %while.64 = (s32[]{:T(128)}, bf16[8,3,64,256]{3,2,1,0:T(8,128)(2,1)}, bf16[8,3,64,2048]{3,2,1,0:T(8,128)(2,1)}, s32[8,3,32]{2,0,1:T(8,128)S(1)}, bf16[48,64,256]{2,1,0:T(8,128)(2,1)}, /*index=5*/s32[]{:T(128)}) while((s32[]{:T(128)}, bf16[8,3,64,256]{3,2,1,0:T(8,128)(2,1)}, bf16[8,3,64,2048]{3,2,1,0:T(8,128)(2,1)}, ...), condition=%wide.region_13.14_spmd, body=%wide.region_12.13_spmd.sunk | while | flops 201327904 | bytes 10427721 | solution.py:69
  502.4 14.8 %all_to_all.79 = bf16[8,192,256]{2,1,0:T(8,128)(2,1)S(1)} all-to-all(bf16[8,192,256]{2,1,0:T(8,128)(2,1)} %bitcast.177), channel_id=1, replica_groups=mesh['row'=16,'col'=8] {'col'}, dimensions={0} | all-to-all | bytes 1572864 | tf_op jit(solution)/shard_map/all_to_all | solution.py:37
  518.2 28.5 %all_to_all.80 = bf16[16,192,256]{2,1,0:T(8,128)(2,1)} all-to-all(bf16[16,192,256]{2,1,0:T(8,128)(2,1)S(1)} %broadcast_in_dim.69), channel_id=1, replica_groups=mesh['row'=16,'col'=8] {'row'}, dimensions={0} | all-to-all | bytes 3145728 | tf_op jit(solution)/shard_map/all_to_all | solution.py:15
  547.7 37.9 %while.65 = (s32[]{:T(128)}, bf16[8,3,64,256]{3,2,1,0:T(8,128)(2,1)}, bf16[8,3,64,2048]{3,2,1,0:T(8,128)(2,1)}, s32[8,3,32]{2,0,1:T(8,128)S(1)}, bf16[48,64,256]{2,1,0:T(8,128)(2,1)}, /*index=5*/s32[]{:T(128)}) while((s32[]{:T(128)}, bf16[8,3,64,256]{3,2,1,0:T(8,128)(2,1)}, bf16[8,3,64,2048]{3,2,1,0:T(8,128)(2,1)}, ...), condition=%wide.region_16.17_spmd, body=%wide.region_15.16_spmd.sunk | while | flops 201327904 | bytes 10427721 | solution.py:69
  585.6 14.7 %all_to_all.81 = bf16[8,192,256]{2,1,0:T(8,128)(2,1)S(1)} all-to-all(bf16[8,192,256]{2,1,0:T(8,128)(2,1)} %bitcast.172), channel_id=1, replica_groups=mesh['row'=16,'col'=8] {'col'}, dimensions={0} | all-to-all | bytes 1572864 | tf_op jit(solution)/shard_map/all_to_all | solution.py:37
  (290 shorter events, 262.5 us)
Async XLA Ops:
  0.0 82.7 %copy-start.3 = (bf16[192,256]{1,0:T(8,128)(2,1)S(1)}, bf16[192,256]{1,0:T(8,128)(2,1)}, u32[]{:S(2)}) copy-start(bf16[192,256]{1,0:T(8,128)(2,1)} %param.18) | copy-start | bytes 294916
  82.7 6.5 %copy-start.5 = (s32[1,1,24,16]{2,3,1,0:T(8,128)S(1)}, s32[1,1,24,16]{2,3,1,0:T(8,128)}, u32[]{:S(2)}) copy-start(s32[1,1,24,16]{2,3,1,0:T(8,128)} %param.21) | copy-start | bytes 4612
  82.7 7.5 %copy-start.4 = (s32[1,1,24,16,2]{2,4,3,1,0:T(2,128)S(1)}, s32[1,1,24,16,2]{2,4,3,1,0:T(2,128)}, u32[]{:S(2)}) copy-start(s32[1,1,24,16,2]{2,4,3,1,0:T(2,128)} %param.20) | copy-start | bytes 9220
  84.0 34.2 %all-to-all-start.1 = ((bf16[16,192,256]{2,1,0:T(8,128)(2,1)}), bf16[16,192,256]{2,1,0:T(8,128)(2,1)}, u32[]{:S(2)}, u32[]{:S(2)}) async-start(bf16[16,192,256]{2,1,0:T(8,128)(2,1)} %broadcast_in_dim.64), calls=%async_computation.1 | async-start | bytes 3145728 | tf_op jit(solution)/shard_map/all_to_all | solution.py:15
  157.0 16.5 %all-to-all-start.2 = ((bf16[8,192,256]{2,1,0:T(8,128)(2,1)}), bf16[8,192,256]{2,1,0:T(8,128)(2,1)S(1)}, u32[]{:S(2)}, u32[]{:S(2)}) async-start(bf16[8,192,256]{2,1,0:T(8,128)(2,1)} %bitcast.173), calls=%async_computation.2 | async-start | bytes 1572864 | tf_op jit(solution)/shard_map/all_to_all | solution.py:37
  175.1 32.0 %all-to-all-start.3 = ((bf16[16,192,256]{2,1,0:T(8,128)(2,1)}), bf16[16,192,256]{2,1,0:T(8,128)(2,1)}, u32[]{:S(2)}, u32[]{:S(2)}) async-start(bf16[16,192,256]{2,1,0:T(8,128)(2,1)} %broadcast_in_dim.65), calls=%async_computation.3 | async-start | bytes 3145728 | tf_op jit(solution)/shard_map/all_to_all | solution.py:15
  263.0 29.5 %all-to-all-start.5 = ((bf16[16,192,256]{2,1,0:T(8,128)(2,1)}), bf16[16,192,256]{2,1,0:T(8,128)(2,1)}, u32[]{:S(2)}, u32[]{:S(2)}) async-start(bf16[16,192,256]{2,1,0:T(8,128)(2,1)} %broadcast_in_dim.66), calls=%async_computation.5 | async-start | bytes 3145728 | tf_op jit(solution)/shard_map/all_to_all | solution.py:15
  348.7 29.4 %all-to-all-start.7 = ((bf16[16,192,256]{2,1,0:T(8,128)(2,1)}), bf16[16,192,256]{2,1,0:T(8,128)(2,1)}, u32[]{:S(2)}, u32[]{:S(2)}) async-start(bf16[16,192,256]{2,1,0:T(8,128)(2,1)} %broadcast_in_dim.67), calls=%async_computation.7 | async-start | bytes 3145728 | tf_op jit(solution)/shard_map/all_to_all | solution.py:15
  379.2 52.8 %copy-start = (f32[192,256]{1,0:T(8,128)S(1)}, f32[192,256]{1,0:T(8,128)}, u32[]{:S(2)}) copy-start(f32[192,256]{1,0:T(8,128)} %get-tuple-element.328) | copy-start | bytes 589828
  434.1 29.4 %all-to-all-start.9 = ((bf16[16,192,256]{2,1,0:T(8,128)(2,1)}), bf16[16,192,256]{2,1,0:T(8,128)(2,1)}, u32[]{:S(2)}, u32[]{:S(2)}) async-start(bf16[16,192,256]{2,1,0:T(8,128)(2,1)} %broadcast_in_dim.68), calls=%async_computation.9 | async-start | bytes 3145728 | tf_op jit(solution)/shard_map/all_to_all | solution.py:15
  464.5 53.5 %copy-start.1 = (f32[192,256]{1,0:T(8,128)S(1)}, f32[192,256]{1,0:T(8,128)}, u32[]{:S(2)}) copy-start(f32[192,256]{1,0:T(8,128)} %get-tuple-element.324) | copy-start | bytes 589828
  517.3 0.7 copy-start.2
where the time goes:
time: 608 us; the launch traced here: 602 us
  blocking collectives  185 us (30%)
  local copies, waits for them, and re-layouts  146 us (24%)
  matrix products  115 us (19%)
  waiting for transfers between devices  103 us (17%)
  starting transfers between devices  37.4 us (6%)
  other arithmetic  12.7 us (2%)
    dot_general x48, matrix products, group_rows(): jnp.einsum('rak,rkv->rav', group_blocks, picked, preferred_element_type=j...  115 us
    gather x48, local copies, waits for them, and re-layouts, group_rows(): gathered[group_columns]  106 us
    all_to_all x5, waiting for transfers between devices, from_everyone(): return lax.all_to_all(copies, axis, split_axis=0, concat_axis=0, tiled=True)  92.6 us
    all_to_all x1, blocking collectives, body(): lax.all_to_all(h_blocks, 'row', split_axis=1, concat_axis=4, tiled=True)  82.7 us
    all_to_all x5, blocking collectives, summed_on_arrival(): lax.all_to_all(blocks, axis, split_axis=0, concat_axis=0, tiled=True)  74 us
    all_to_all x5, starting transfers between devices, from_everyone(): return lax.all_to_all(copies, axis, split_axis=0, concat_axis=0, tiled=True)  32.9 us
    all_to_all x1, blocking collectives, from_everyone(): return lax.all_to_all(copies, axis, split_axis=0, concat_axis=0, tiled=True)  28.5 us
  transfers between devices with their start and end apart: 6, of which 5 were waited for; matrix products, arithmetic and copies ran while one was open for 5% of the time, Pallas kernels for 0%

commit v1 on v0

v1 whole, which is shorter than its diff:
```python
import jax
import jax.numpy as jnp
from jax import lax
from jax.experimental import pallas as pl
from jax.experimental.pallas import tpu as pltpu
from jax.sharding import PartitionSpec as P

BLOCK = 64
VECTORS = 256
PER = 2
DEGREE = 6
BLOCK_ROWS = 3
N_ROW = 16
N_COL = 8
OWN = BLOCK_ROWS * BLOCK
DOMAIN = BLOCK_ROWS * N_COL
ROWS = DOMAIN * BLOCK
CHUNKS = 4
CHUNK = 4 * OWN
MESH = pl.DeviceIdType.MESH


def flip(value):
    return value + 1 - 2 * (value % 2)


def kernel(
    coef_ref,
    scal_ref,
    trial_ref,
    h_ref,
    out_ref,
    hbuf,
    dense,
    gathered,
    total,
    partial,
    arrived,
    current,
    previous,
    h_send,
    h_recv,
    own_sem,
    g_send,
    f_send,
    g_recv,
    p_send,
    p_recv,
):
    row, col = lax.axis_index("row"), lax.axis_index("col")
    core, y, zh = row % 2, (row // 2) % 4, row // 8
    x, zl = col // 2, col % 2
    mate = flip(row)

    def pair_y(j):
        base = y if j < 2 else (y + 2) % 4
        return flip(base) if j % 2 else base

    chips = [(zh if m < 4 else 1 - zh, pair_y(m % 4)) for m in range(8)]
    same_core = [a * 8 + b * 2 + core for a, b in chips]
    other_core = [a * 8 + b * 2 + 1 - core for a, b in chips]
    cols = [((x + j) % 4) * 2 + k for j in range(4) for k in range(2)]

    barrier = pltpu.get_barrier_semaphore()
    row_peers = same_core[1:] + other_core
    for peer in row_peers:
        pl.semaphore_signal(barrier, inc=1, device_id=(peer, col), device_id_type=MESH)
    for j in range(1, N_COL):
        pl.semaphore_signal(
            barrier, inc=1, device_id=(row, (col + j) % N_COL), device_id_type=MESH
        )
    pl.semaphore_wait(barrier, len(row_peers) + N_COL - 1)

    def v_slot(p, s):
        return gathered.at[p, s // 4, pl.ds(pl.multiple_of((s % 4) * OWN, OWN), OWN), :]

    def v_copy(p, s, sem, to):
        return pltpu.make_async_remote_copy(
            src_ref=v_slot(p, s),
            dst_ref=v_slot(p, s),
            send_sem=sem,
            recv_sem=g_recv.at[p, s],
            device_id=(to, col),
            device_id_type=MESH,
        )

    def start_gather(p):
        v_copy(p, row, g_send.at[0], mate).start()
        for m in (1, 3, 2, 4, 5, 7, 6):
            v_copy(p, row, g_send.at[m], same_core[m]).start()

    current[...] = trial_ref[...].astype(jnp.float32)
    previous[...] = jnp.zeros_like(previous)
    gathered[0, row // 4, pl.ds(pl.multiple_of((row % 4) * OWN, OWN), OWN), :] = trial_ref[...]
    start_gather(0)

    def h_copy(i, to):
        return pltpu.make_async_remote_copy(
            src_ref=h_ref.at[to],
            dst_ref=hbuf.at[row],
            send_sem=h_send.at[i],
            recv_sem=h_recv.at[row],
            device_id=(to, col),
            device_id_type=MESH,
        )

    for i, peer in enumerate(row_peers):
        h_copy(i, peer).start()
    own = pltpu.make_async_copy(h_ref.at[row], hbuf.at[row], own_sem)
    own.start()
    own.wait()

    def h_wait(s):
        pltpu.make_async_remote_copy(
            src_ref=h_ref.at[0],
            dst_ref=hbuf.at[s],
            send_sem=h_send.at[0],
            recv_sem=h_recv.at[s],
            device_id=(mate, col),
            device_id_type=MESH,
        ).wait_recv()

    left = lax.broadcasted_iota(jnp.int32, (BLOCK, 2 * BLOCK), 1) < BLOCK

    def expand(pair):
        even, odd = pair * 2, pair * 2 + 1

        def one(i, carry):
            def coef(s, q, j):
                return coef_ref[((i * N_ROW + s) * PER + q) * BLOCK_ROWS + j]

            def lanes(a, b):
                return jnp.where(left, a, b)

            be = hbuf[even, i].astype(jnp.float32)
            bo = hbuf[odd, i].astype(jnp.float32)
            re, ro = pltpu.roll(be, BLOCK, 1), pltpu.roll(bo, BLOCK, 1)
            first = be * lanes(coef(even, 0, 0), coef(even, 1, 1)) + re * lanes(
                coef(even, 1, 0), coef(even, 0, 1)
            )
            middle = jnp.where(
                left,
                be * coef(even, 0, 2) + re * coef(even, 1, 2),
                bo * coef(odd, 1, 0) + ro * coef(odd, 0, 0),
            )
            last = bo * lanes(coef(odd, 0, 1), coef(odd, 1, 2)) + ro * lanes(
                coef(odd, 1, 1), coef(odd, 0, 2)
            )
            at = pl.ds(pl.multiple_of(i * BLOCK, BLOCK), BLOCK)
            offset = (pair % 2) * (2 * OWN)
            for k, part in enumerate((first, middle, last)):
                dense[
                    pair // 2,
                    at,
                    pl.ds(pl.multiple_of(offset + k * 2 * BLOCK, 2 * BLOCK), 2 * BLOCK),
                ] = part.astype(jnp.bfloat16)
            return carry

        lax.fori_loop(0, DOMAIN, one, 0)

    for m in range(8):
        if m > 0:
            h_wait(same_core[m])
        h_wait(other_core[m])
        expand(same_core[m] // 2)
    for i, peer in enumerate(row_peers):
        h_copy(i, peer).wait_send()

    center, half = scal_ref[0], scal_ref[1]
    TILE = 2 * OWN

    def step(k, carry):
        p = k % 2

        @pl.when(k > 0)
        def _():
            start_gather(p)

        def product(m, rows_at):
            chunk = same_core[2 * m] // 4
            return jnp.dot(
                dense[chunk, rows_at, :],
                gathered[p, chunk],
                preferred_element_type=jnp.float32,
            )

        for m in range(CHUNKS):
            for n in (2 * m, 2 * m + 1):
                if n > 0:
                    v_copy(p, same_core[n], f_send.at[n], mate).wait_recv()
                    v_copy(p, same_core[n], f_send.at[n], mate).start()
            for n in (2 * m, 2 * m + 1):
                v_copy(p, other_core[n], f_send.at[n], mate).wait_recv()
            if m < CHUNKS - 1:

                def tile(t, c, m=m):
                    at = pl.ds(pl.multiple_of(t * TILE, TILE), TILE)
                    if m == 0:
                        total[at, :] = product(m, at)
                    else:
                        total[at, :] += product(m, at)
                    return c

                lax.fori_loop(0, ROWS // TILE, tile, 0)

        def p_copy(n):
            return pltpu.make_async_remote_copy(
                src_ref=partial.at[cols[n]],
                dst_ref=arrived.at[p, col],
                send_sem=p_send.at[n],
                recv_sem=p_recv.at[p, col],
                device_id=(row, cols[n]),
                device_id_type=MESH,
            )

        def p_exchange(n, act):
            if n >= 2:
                act(p_copy(n))
            else:

                @pl.when(zl != n)
                def _():
                    act(p_copy(n))

        for j in (1, 3, 2, 0):
            xx = (x + j) % 4
            at = pl.ds(pl.multiple_of(xx * TILE, TILE), TILE)
            value = (total[at, :] + product(CHUNKS - 1, at)).astype(jnp.bfloat16)
            partial[pl.ds(xx * 2, 2)] = value.reshape(2, OWN, VECTORS)
            for n in (2 * j, 2 * j + 1):
                p_exchange(n, lambda c: c.start())

        for m in range(7):
            v_copy(p, row, g_send.at[m + 1], same_core[m + 1]).wait_send()
            v_copy(p, same_core[m + 1], f_send.at[m + 1], mate).wait_send()
        v_copy(p, row, g_send.at[0], mate).wait_send()

        arrived[p, col] = partial[col]
        for j in range(1, N_COL):
            s = (col + j) % N_COL
            pltpu.make_async_remote_copy(
                src_ref=partial.at[s],
                dst_ref=arrived.at[p, s],
                send_sem=p_send.at[0],
                recv_sem=p_recv.at[p, s],
                device_id=(row, s),
                device_id_type=MESH,
            ).wait_recv()
        for n in range(N_COL):
            p_exchange(n, lambda c: c.wait_send())

        applied = arrived[p, 0].astype(jnp.float32)
        for s in range(1, N_COL):
            applied = applied + arrived[p, s].astype(jnp.float32)
        now = current[...]
        scale = jnp.where(k == 0, 1.0, 2.0)
        following = scale * (applied - center * now) / half - previous[...]
        previous[...] = now
        current[...] = following
        gathered[1 - p, row // 4, pl.ds(pl.multiple_of((row % 4) * OWN, OWN), OWN), :] = (
            following.astype(jnp.bfloat16)
        )
        return carry

    lax.fori_loop(0, DEGREE, step, 0)
    out_ref[...] = current[...]


def body(trial_vectors, h_blocks, block_col, block_count, center, half_width):
    slot = lax.broadcasted_iota(jnp.int32, (DOMAIN, N_ROW, PER), 2)
    filled = slot < block_count[0, 0][:, :, None]
    code = jnp.where(filled, block_col[0, 0], -1)
    coef = (code[..., None] == jnp.arange(BLOCK_ROWS, dtype=jnp.int32)).astype(jnp.float32)
    scal = jnp.concatenate([center, half_width])
    vmem, smem = (
        pl.BlockSpec(memory_space=pltpu.VMEM),
        pl.BlockSpec(memory_space=pltpu.SMEM),
    )
    dma = pltpu.SemaphoreType.DMA
    bf16, f32 = jnp.bfloat16, jnp.float32
    return pl.pallas_call(
        kernel,
        out_shape=jax.ShapeDtypeStruct((OWN, VECTORS), f32),
        in_specs=[smem, smem, vmem, pl.BlockSpec(memory_space=pl.ANY)],
        out_specs=vmem,
        scratch_shapes=[
            pltpu.VMEM((N_ROW, DOMAIN, BLOCK, PER * BLOCK), bf16),
            pltpu.VMEM((CHUNKS, ROWS, CHUNK), bf16),
            pltpu.VMEM((2, CHUNKS, CHUNK, VECTORS), bf16),
            pltpu.VMEM((ROWS, VECTORS), f32),
            pltpu.VMEM((N_COL, OWN, VECTORS), bf16),
            pltpu.VMEM((2, N_COL, OWN, VECTORS), bf16),
            pltpu.VMEM((OWN, VECTORS), f32),
            pltpu.VMEM((OWN, VECTORS), f32),
            dma((N_ROW,)),
            dma((N_ROW,)),
            dma,
            dma((8,)),
            dma((8,)),
            dma((2, N_ROW)),
            dma((N_COL,)),
            dma((2, N_COL)),
        ],
        compiler_params=pltpu.CompilerParams(
            collective_id=0, has_side_effects=True, vmem_limit_bytes=48 * 2**20
        ),
        name="filter",
    )(coef.reshape(-1), scal, trial_vectors, h_blocks[0, :, :, :, 0, :])


def solution(mesh):
    in_specs = (
        P(("row", "col"), None),
        P("col", None, None, None, "row", None),
        P("col", "row", None, None, None),
        P("col", "row", None, None),
        P(),
        P(),
    )
    out_specs = P(("row", "col"), None)
    return jax.shard_map(body, mesh=mesh, in_specs=in_specs, out_specs=out_specs, check_vma=False)
```

time: 608 us -> 266 us (0.44)
  Pallas kernels: 0 us -> 261 us
  blocking collectives: 185 us -> 0 us
  local copies, waits for them, and re-layouts: 146 us -> 2.24 us
  matrix products: 115 us -> 0 us
  waiting for transfers between devices: 103 us -> 0 us
  starting transfers between devices: 37.4 us -> 0 us
  other arithmetic: 12.7 us -> 1.38 us
    pallas_call x0 -> x1, Pallas kernels: none -> 261 us  [body(): pl.pallas_call(kernel, out_shape=jax.ShapeDtypeStruct((OWN, VECTORS), f32...]
    all_to_all x7 -> x0, blocking collectives: 185 us -> none  [the longest x1 82.7 us: body(): lax.all_to_all(h_blocks, 'row', split_axis=1, concat_axis=4, tiled=True)]
    dot_general x48 -> x0, matrix products: 115 us -> none  [group_rows(): jnp.einsum('rak,rkv->rav', group_blocks, picked, preferred_element_type=j...]
    gather x48 -> x0, local copies, waits for them, and re-layouts: 106 us -> none  [group_rows(): gathered[group_columns]]
    all_to_all x6 -> x0, waiting for transfers between devices: 103 us -> none  [the longest x5 92.6 us: from_everyone(): return lax.all_to_all(copies, axis, split_axis=0, concat_axis=0, tiled=True)]
    all_to_all x6 -> x0, starting transfers between devices: 37.4 us -> none  [the longest x5 32.9 us: from_everyone(): return lax.all_to_all(copies, axis, split_axis=0, concat_axis=0, tiled=True)]
    another operation x7 -> x0, local copies, waits for them, and re-layouts: 16.4 us -> none  [the longest x1 10.3 us: body(): shaped = arrived[0, 0].reshape(domain, BLOCK, row_count, PER, BLOCK)]
    all_to_all x1 -> x0, local copies, waits for them, and re-layouts: 11.1 us -> none  [body(): lax.all_to_all(h_blocks, 'row', split_axis=1, concat_axis=4, tiled=True)]
  transfers between devices with their start and end apart: 6 -> 0, of which waited for: 5 -> 0; matrix products, arithmetic and copies ran while one was open for 5% -> 0% of each run, Pallas kernels for 0% -> 0%
where the time goes in v1:
time: 266 us
  Pallas kernels  261 us (98%)
    pallas_call x1, Pallas kernels, body(): pl.pallas_call(kernel, out_shape=jax.ShapeDtypeStruct((OWN, VECTORS), f32...  261 us

profile of v1, /device:TPU:1, one launch (start us, length us, event | category | flops | bytes accessed | tf_op | source)
XLA Modules:
  0.0 265.7 jit_solution(1905220717243792429)
XLA Ops:
  0.0 0.7 compare_select_fusion
  0.7 0.2 copy.8
  0.9 0.6 compare_convert_fusion
  1.5 0.5 reshape.16.coef_ref
  3.3 0.1 pad_maximum_fusion.scal_ref
  3.4 0.0 copy-start
  3.4 0.9 copy-done
  4.3 260.8 %filter.1 = f32[192,256]{1,0:T(8,128)S(1)} custom-call(f32[2304]{0:T(1024)S(1)} %reshape.16.coef_ref, f32[2]{0:T(128)S(1)} %pad_maximum_fusion.scal_ref, bf16[192,256]{1,0:T(8,128)(2,1)S(1)} %copy-done, bf16[16,24,64,128]{3,2,1,0:T(8,128)(2,1)} %bitcast.4), custom_call_target="tpu_custom_call" | custom-call | tf_op jit(solution)/shard_map/filter/pallas_call | solution.py:281
  265.1 0.7 copy.12
Async XLA Ops:
  3.4 0.9 copy-start

commit v2 on v1

v2 whole, which is shorter than its diff:
```python
import jax
import jax.numpy as jnp
from jax import lax
from jax.experimental import pallas as pl
from jax.experimental.pallas import tpu as pltpu
from jax.sharding import PartitionSpec as P

BLOCK = 64
VECTORS = 256
PER = 2
DEGREE = 6
BLOCK_ROWS = 3
N_ROW = 16
N_COL = 8
OWN = BLOCK_ROWS * BLOCK
DOMAIN = BLOCK_ROWS * N_COL
ROWS = DOMAIN * BLOCK
CHIPS = 8
CHUNKS = 4
CHUNK = 4 * OWN
PIECES = 8
PIECE = DOMAIN // PIECES
MESH = pl.DeviceIdType.MESH
GATHER_ORDER = (1, 3, 2, 4, 5, 7, 6)
H_ORDER = (
    (1, 0, 0), (0, 1, 0), (0, 3, 0), (1, 0, 1), (0, 1, 1), (0, 3, 1), (1, 2, 0), (0, 2, 0),
    (1, 2, 1), (0, 2, 1), (1, 1, 0), (1, 3, 0), (1, 1, 1), (1, 3, 1), (0, 0, 1),
)
SCATTER_ORDER = ((2, 1), (3, 1), (2, 0), (3, 0), (1, 1), (0, 1), (1, 0))
SCATTER_READY = ((0, 1, 2, 3), (4, 5, 6))


def flip(value):
    return value + 1 - 2 * (value % 2)


def kernel(
    coef_ref,
    scal_ref,
    trial_ref,
    h_ref,
    out_ref,
    hbuf,
    dense,
    gathered,
    total,
    partial,
    arrived,
    current,
    previous,
    h_send,
    h_recv,
    g_send,
    f_send,
    g_recv,
    p_send,
    p_recv,
):
    row, col = lax.axis_index("row"), lax.axis_index("col")
    core, y, zh = row % 2, (row // 2) % 4, row // 8
    x, zl = col // 2, col % 2
    mate = flip(row)

    def chip(dz, dy, dc=0):
        return ((zh + dz) % 2) * 8 + ((y + dy) % 4) * 2 + (core + dc) % 2

    def pair_y(j):
        base = y if j < 2 else (y + 2) % 4
        return flip(base) if j % 2 else base

    same_core = [
        (zh if m < 4 else 1 - zh) * 8 + pair_y(m % 4) * 2 + core for m in range(CHIPS)
    ]

    barrier = pltpu.get_barrier_semaphore()
    for step_to in H_ORDER:
        pl.semaphore_signal(
            barrier, inc=1, device_id=(chip(*step_to), col), device_id_type=MESH
        )
    for j in range(1, N_COL):
        pl.semaphore_signal(
            barrier, inc=1, device_id=(row, (col + j) % N_COL), device_id_type=MESH
        )
    pl.semaphore_wait(barrier, N_ROW + N_COL - 2)

    def v_slot(p, s):
        return gathered.at[p, s // 4, pl.ds(pl.multiple_of((s % 4) * OWN, OWN), OWN), :]

    def v_copy(p, s, sem, to):
        return pltpu.make_async_remote_copy(
            src_ref=v_slot(p, s),
            dst_ref=v_slot(p, s),
            send_sem=sem,
            recv_sem=g_recv.at[p, s],
            device_id=(to, col),
            device_id_type=MESH,
        )

    def start_gather(p):
        v_copy(p, row, g_send.at[0], mate).start()
        for m in GATHER_ORDER:
            v_copy(p, row, g_send.at[m], same_core[m]).start()

    current[...] = trial_ref[...].astype(jnp.float32)
    previous[...] = jnp.zeros_like(previous)
    gathered[0, row // 4, pl.ds(pl.multiple_of((row % 4) * OWN, OWN), OWN), :] = trial_ref[...]
    start_gather(0)

    def h_copy(i, n, to):
        return pltpu.make_async_remote_copy(
            src_ref=h_ref.at[to, pl.ds(i * PIECE, PIECE)],
            dst_ref=hbuf.at[i, row],
            send_sem=h_send.at[i, n],
            recv_sem=h_recv.at[i],
            device_id=(to, col),
            device_id_type=MESH,
        )

    def h_own(i):
        return pltpu.make_async_copy(
            h_ref.at[row, pl.ds(i * PIECE, PIECE)], hbuf.at[i, row], h_recv.at[i]
        )

    def h_start(i, c):
        for n, step_to in enumerate(H_ORDER):
            h_copy(i, n, chip(*step_to)).start()
        h_own(i).start()
        return c

    lax.fori_loop(0, PIECES, h_start, 0)

    left = lax.broadcasted_iota(jnp.int32, (BLOCK, 2 * BLOCK), 1) < BLOCK

    def expand(piece, pair):
        even, odd = pair * 2, pair * 2 + 1

        def one(at_piece, carry):
            i = piece * PIECE + at_piece

            def coef(s, q, j):
                return coef_ref[((i * N_ROW + s) * PER + q) * BLOCK_ROWS + j]

            def lanes(a, b):
                return jnp.where(left, a, b)

            be = hbuf[piece, even, at_piece].astype(jnp.float32)
            bo = hbuf[piece, odd, at_piece].astype(jnp.float32)
            re, ro = pltpu.roll(be, BLOCK, 1), pltpu.roll(bo, BLOCK, 1)
            first = be * lanes(coef(even, 0, 0), coef(even, 1, 1)) + re * lanes(
                coef(even, 1, 0), coef(even, 0, 1)
            )
            middle = jnp.where(
                left,
                be * coef(even, 0, 2) + re * coef(even, 1, 2),
                bo * coef(odd, 1, 0) + ro * coef(odd, 0, 0),
            )
            last = bo * lanes(coef(odd, 0, 1), coef(odd, 1, 2)) + ro * lanes(
                coef(odd, 1, 1), coef(odd, 0, 2)
            )
            at = pl.ds(pl.multiple_of(i * BLOCK, BLOCK), BLOCK)
            offset = (pair % 2) * (2 * OWN)
            for k, part in enumerate((first, middle, last)):
                dense[
                    pair // 2,
                    at,
                    pl.ds(pl.multiple_of(offset + k * 2 * BLOCK, 2 * BLOCK), 2 * BLOCK),
                ] = part.astype(jnp.bfloat16)
            return carry

        lax.fori_loop(0, PIECE, one, 0)

    def h_arrive(i, c):
        pltpu.make_async_copy(hbuf.at[i], hbuf.at[i], h_recv.at[i]).wait()

        def one_pair(pair, cc):
            expand(i, pair)
            return cc

        lax.fori_loop(0, N_ROW // 2, one_pair, 0)
        return c

    lax.fori_loop(0, PIECES, h_arrive, 0)

    def h_sent(i, c):
        for n, step_to in enumerate(H_ORDER):
            h_copy(i, n, chip(*step_to)).wait_send()
        return c

    lax.fori_loop(0, PIECES, h_sent, 0)

    center, half = scal_ref[0], scal_ref[1]
    HALF = ROWS // 2

    def step(k, carry):
        p = k % 2

        @pl.when(k > 0)
        def _():
            start_gather(p)

        def product(chunk, rows_at):
            return jnp.dot(
                dense[chunk, rows_at, :],
                gathered[p, chunk],
                preferred_element_type=jnp.float32,
            )

        here = {0}
        done = 0
        for m in GATHER_ORDER:
            v_copy(p, same_core[m], f_send.at[m], mate).wait_recv()
            v_copy(p, same_core[m], f_send.at[m], mate).start()
            here.add(m)
            if m ^ 1 in here:
                for n in (m, m ^ 1):
                    v_copy(p, flip(same_core[n]), f_send.at[n], mate).wait_recv()
                chunk = same_core[m] // 4
                done += 1
                if done == 1:
                    total[...] = product(chunk, slice(None))
                elif done < CHUNKS:
                    total[...] += product(chunk, slice(None))

        def p_copy(n):
            j, dl = SCATTER_ORDER[n]
            base = x if j < 2 else (x + 2) % 4
            to = (flip(base) if j % 2 else base) * 2 + (zl + dl) % 2
            return pltpu.make_async_remote_copy(
                src_ref=partial.at[to],
                dst_ref=arrived.at[p, col],
                send_sem=p_send.at[n],
                recv_sem=p_recv.at[p, col],
                device_id=(row, to),
                device_id_type=MESH,
            )

        for half_at, ready in enumerate(SCATTER_READY):
            first = (x // 2 + 1 + half_at) % 2
            at = pl.ds(pl.multiple_of(first * HALF, HALF), HALF)
            value = (total[at, :] + product(chunk, at)).astype(jnp.bfloat16)
            partial[pl.ds(first * 4, 4)] = value.reshape(4, OWN, VECTORS)
            for n in ready:
                p_copy(n).start()

        v_copy(p, row, g_send.at[0], mate).wait_send()
        for m in range(1, CHIPS):
            v_copy(p, row, g_send.at[m], mate).wait_send()
            v_copy(p, same_core[m], f_send.at[m], mate).wait_send()

        arrived[p, col] = partial[col]
        for j in range(1, N_COL):
            s = (col + j) % N_COL
            pltpu.make_async_remote_copy(
                src_ref=partial.at[s],
                dst_ref=arrived.at[p, s],
                send_sem=p_send.at[0],
                recv_sem=p_recv.at[p, s],
                device_id=(row, s),
                device_id_type=MESH,
            ).wait_recv()
        for n in range(N_COL - 1):
            p_copy(n).wait_send()

        applied = arrived[p, 0].astype(jnp.float32)
        for s in range(1, N_COL):
            applied = applied + arrived[p, s].astype(jnp.float32)
        now = current[...]
        scale = jnp.where(k == 0, 1.0, 2.0)
        following = scale * (applied - center * now) / half - previous[...]
        previous[...] = now
        current[...] = following
        gathered[1 - p, row // 4, pl.ds(pl.multiple_of((row % 4) * OWN, OWN), OWN), :] = (
            following.astype(jnp.bfloat16)
        )
        return carry

    lax.fori_loop(0, DEGREE, step, 0)
    out_ref[...] = current[...]


def body(trial_vectors, h_blocks, block_col, block_count, center, half_width):
    slot = lax.broadcasted_iota(jnp.int32, (DOMAIN, N_ROW, PER), 2)
    filled = slot < block_count[0, 0][:, :, None]
    code = jnp.where(filled, block_col[0, 0], -1)
    coef = (code[..., None] == jnp.arange(BLOCK_ROWS, dtype=jnp.int32)).astype(jnp.float32)
    scal = jnp.concatenate([center, half_width])
    vmem, smem = (
        pl.BlockSpec(memory_space=pltpu.VMEM),
        pl.BlockSpec(memory_space=pltpu.SMEM),
    )
    dma = pltpu.SemaphoreType.DMA
    bf16, f32 = jnp.bfloat16, jnp.float32
    return pl.pallas_call(
        kernel,
        out_shape=jax.ShapeDtypeStruct((OWN, VECTORS), f32),
        in_specs=[smem, smem, vmem, pl.BlockSpec(memory_space=pl.ANY)],
        out_specs=vmem,
        scratch_shapes=[
            pltpu.VMEM((PIECES, N_ROW, PIECE, BLOCK, PER * BLOCK), bf16),
            pltpu.VMEM((CHUNKS, ROWS, CHUNK), bf16),
            pltpu.VMEM((2, CHUNKS, CHUNK, VECTORS), bf16),
            pltpu.VMEM((ROWS, VECTORS), f32),
            pltpu.VMEM((N_COL, OWN, VECTORS), bf16),
            pltpu.VMEM((2, N_COL, OWN, VECTORS), bf16),
            pltpu.VMEM((OWN, VECTORS), f32),
            pltpu.VMEM((OWN, VECTORS), f32),
            dma((PIECES, N_ROW - 1)),
            dma((PIECES,)),
            dma((CHIPS,)),
            dma((CHIPS,)),
            dma((2, N_ROW)),
            dma((N_COL - 1,)),
            dma((2, N_COL)),
        ],
        compiler_params=pltpu.CompilerParams(
            collective_id=0, has_side_effects=True, vmem_limit_bytes=48 * 2**20
        ),
        name="filter",
    )(coef.reshape(-1), scal, trial_vectors, h_blocks[0, :, :, :, 0, :])


def solution(mesh):
    in_specs = (
        P(("row", "col"), None),
        P("col", None, None, None, "row", None),
        P("col", "row", None, None, None),
        P("col", "row", None, None),
        P(),
        P(),
    )
    out_specs = P(("row", "col"), None)
    return jax.shard_map(body, mesh=mesh, in_specs=in_specs, out_specs=out_specs, check_vma=False)
```

time: 266 us -> 250 us (0.940)
  Pallas kernels: 261 us -> 245 us
    pallas_call x1, Pallas kernels: 261 us -> 245 us  [body(): pl.pallas_call(kernel, out_shape=jax.ShapeDtypeStruct((OWN, VECTORS), f32...]
where the time goes in v2:
time: 250 us
  Pallas kernels  245 us (98%)
    pallas_call x1, Pallas kernels, body(): pl.pallas_call(kernel, out_shape=jax.ShapeDtypeStruct((OWN, VECTORS), f32...  245 us

profile of v2, /device:TPU:1, one launch (start us, length us, event | category | flops | bytes accessed | tf_op | source)
XLA Modules:
  0.0 249.8 jit_solution(11561297156629683486)
XLA Ops:
  0.0 0.7 compare_select_fusion
  0.7 0.2 copy.8
  0.9 0.6 compare_convert_fusion
  1.5 0.5 reshape.16.coef_ref
  3.3 0.1 pad_maximum_fusion.scal_ref
  3.4 0.0 copy-start
  3.4 0.9 copy-done
  4.3 244.9 %filter.1 = f32[192,256]{1,0:T(8,128)S(1)} custom-call(f32[2304]{0:T(1024)S(1)} %reshape.16.coef_ref, f32[2]{0:T(128)S(1)} %pad_maximum_fusion.scal_ref, bf16[192,256]{1,0:T(8,128)(2,1)S(1)} %copy-done, bf16[16,24,64,128]{3,2,1,0:T(8,128)(2,1)} %bitcast.4), custom_call_target="tpu_custom_call" | custom-call | tf_op jit(solution)/shard_map/filter/pallas_call | solution.py:293
  249.1 0.7 copy.12
Async XLA Ops:
  3.4 0.9 copy-start

commit v3 on v2

--- a/solution.py
+++ b/solution.py
@@ -12,16 +12,20 @@
 BLOCK_ROWS = 3
 N_ROW = 16
 N_COL = 8
+WIDTH = VECTORS // 2
+TURNS = 2 * DEGREE
 OWN = BLOCK_ROWS * BLOCK
 DOMAIN = BLOCK_ROWS * N_COL
 ROWS = DOMAIN * BLOCK
 CHIPS = 8
-CHUNKS = 4
-CHUNK = 4 * OWN
+CHUNK = 8 * OWN
 PIECES = 8
 PIECE = DOMAIN // PIECES
 MESH = pl.DeviceIdType.MESH
-GATHER_ORDER = (1, 3, 2, 4, 5, 7, 6)
+GATHER_ORDER = (4, 1, 3, 2)
+RELAY_ORDER = (1, 3, 2)
+ARRIVAL_ORDER = (4, 1, 3, 2, 5, 7, 6)
+FINISH_AT = 4
 H_ORDER = (
     (1, 0, 0), (0, 1, 0), (0, 3, 0), (1, 0, 1), (0, 1, 1), (0, 3, 1), (1, 2, 0), (0, 2, 0),
     (1, 2, 1), (0, 2, 1), (1, 1, 0), (1, 3, 0), (1, 1, 1), (1, 3, 1), (0, 0, 1),
@@ -51,7 +55,9 @@
     h_send,
     h_recv,
     g_send,
+    r_send,
     f_send,
+    f_recv,
     g_recv,
     p_send,
     p_recv,
@@ -83,28 +89,53 @@
         )
     pl.semaphore_wait(barrier, N_ROW + N_COL - 2)
 
-    def v_slot(p, s):
-        return gathered.at[p, s // 4, pl.ds(pl.multiple_of((s % 4) * OWN, OWN), OWN), :]
-
-    def v_copy(p, s, sem, to):
+    def v_rows(s):
+        place = (s % 2) * 4 + (s // 2) % 4
+        return pl.ds(pl.multiple_of(place * OWN, OWN), OWN)
+
+    def v_slot(b, s):
+        return gathered.at[b, s // 8, v_rows(s), :]
+
+    def v_copy(b, s, sem, to):
         return pltpu.make_async_remote_copy(
-            src_ref=v_slot(p, s),
-            dst_ref=v_slot(p, s),
+            src_ref=v_slot(b, s),
+            dst_ref=v_slot(b, s),
             send_sem=sem,
-            recv_sem=g_recv.at[p, s],
+            recv_sem=g_recv.at[b, s // 2],
             device_id=(to, col),
             device_id_type=MESH,
         )
 
-    def start_gather(p):
-        v_copy(p, row, g_send.at[0], mate).start()
+    def share(b, m):
+        s = same_core[m]
+        return pltpu.make_async_remote_copy(
+            src_ref=v_slot(b, s),
+            dst_ref=v_slot(b, s),
+            send_sem=f_send.at[b % 2, m],
+            recv_sem=f_recv.at[b, s // 8],
+            device_id=(mate, col),
+            device_id_type=MESH,
+        )
+
+    def shared(b, z):
+        half_slot = gathered.at[b, z, pl.ds(pl.multiple_of((1 - core) * 4 * OWN, OWN), 4 * OWN), :]
+        pltpu.make_async_copy(half_slot, half_slot, f_recv.at[b, z]).wait()
+
+    def start_gather(t, value):
+        b, h = t % 4, t % 2
+        gathered[b, zh, v_rows(row), :] = value
         for m in GATHER_ORDER:
-            v_copy(p, row, g_send.at[m], same_core[m]).start()
-
-    current[...] = trial_ref[...].astype(jnp.float32)
+            v_copy(b, row, g_send.at[h, m], same_core[m]).start()
+        share(b, 0).start()
+
+    def relay(b, m):
+        return v_copy(b, same_core[4], r_send.at[m], same_core[m])
+
+    for h in range(2):
+        value = trial_ref[:, h * WIDTH : (h + 1) * WIDTH]
+        current[h] = value.astype(jnp.float32)
+        start_gather(h, value)
     previous[...] = jnp.zeros_like(previous)
-    gathered[0, row // 4, pl.ds(pl.multiple_of((row % 4) * OWN, OWN), OWN), :] = trial_ref[...]
-    start_gather(0)
 
     def h_copy(i, n, to):
         return pltpu.make_async_remote_copy(
@@ -132,7 +163,8 @@
     left = lax.broadcasted_iota(jnp.int32, (BLOCK, 2 * BLOCK), 1) < BLOCK
 
     def expand(piece, pair):
-        even, odd = pair * 2, pair * 2 + 1
+        even = (pair // 4) * 8 + (pair % 2) * 4 + (pair // 2) % 2
+        odd = even + 2
 
         def one(at_piece, carry):
             i = piece * PIECE + at_piece
@@ -158,10 +190,10 @@
                 coef(odd, 1, 1), coef(odd, 0, 2)
             )
             at = pl.ds(pl.multiple_of(i * BLOCK, BLOCK), BLOCK)
-            offset = (pair % 2) * (2 * OWN)
+            offset = (pair % 4) * (2 * OWN)
             for k, part in enumerate((first, middle, last)):
                 dense[
-                    pair // 2,
+                    pair // 4,
                     at,
                     pl.ds(pl.multiple_of(offset + k * 2 * BLOCK, 2 * BLOCK), 2 * BLOCK),
                 ] = part.astype(jnp.bfloat16)
@@ -191,91 +223,103 @@
     center, half = scal_ref[0], scal_ref[1]
     HALF = ROWS // 2
 
-    def step(k, carry):
-        p = k % 2
-
-        @pl.when(k > 0)
-        def _():
-            start_gather(p)
+    def p_copy(t, n):
+        j, dl = SCATTER_ORDER[n]
+        base = x if j < 2 else (x + 2) % 4
+        to = (flip(base) if j % 2 else base) * 2 + (zl + dl) % 2
+        return pltpu.make_async_remote_copy(
+            src_ref=partial.at[t % 2, to],
+            dst_ref=arrived.at[t % 4, col],
+            send_sem=p_send.at[t % 2, n],
+            recv_sem=p_recv.at[t % 4, col],
+            device_id=(row, to),
+            device_id_type=MESH,
+        )
+
+    def multiply(t, finish_other):
+        b, h = t % 4, t % 2
 
         def product(chunk, rows_at):
             return jnp.dot(
                 dense[chunk, rows_at, :],
-                gathered[p, chunk],
+                gathered[b, chunk],
                 preferred_element_type=jnp.float32,
             )
 
-        here = {0}
-        done = 0
-        for m in GATHER_ORDER:
-            v_copy(p, same_core[m], f_send.at[m], mate).wait_recv()
-            v_copy(p, same_core[m], f_send.at[m], mate).start()
-            here.add(m)
-            if m ^ 1 in here:
-                for n in (m, m ^ 1):
-                    v_copy(p, flip(same_core[n]), f_send.at[n], mate).wait_recv()
-                chunk = same_core[m] // 4
-                done += 1
-                if done == 1:
-                    total[...] = product(chunk, slice(None))
-                elif done < CHUNKS:
-                    total[...] += product(chunk, slice(None))
-
-        def p_copy(n):
-            j, dl = SCATTER_ORDER[n]
-            base = x if j < 2 else (x + 2) % 4
-            to = (flip(base) if j % 2 else base) * 2 + (zl + dl) % 2
-            return pltpu.make_async_remote_copy(
-                src_ref=partial.at[to],
-                dst_ref=arrived.at[p, col],
-                send_sem=p_send.at[n],
-                recv_sem=p_recv.at[p, col],
-                device_id=(row, to),
-                device_id_type=MESH,
-            )
+        def arrive(m):
+            v_copy(b, same_core[m], g_send.at[h, 1], mate).wait_recv()
+            if m == 4:
+                for n in RELAY_ORDER:
+                    relay(b, n).start()
+            share(b, m).start()
+
+        for m in ARRIVAL_ORDER[:FINISH_AT]:
+            arrive(m)
+        shared(b, zh)
+        total[...] = product(zh, slice(None))
+        finish_other()
+        for m in ARRIVAL_ORDER[FINISH_AT:]:
+            arrive(m)
+        shared(b, 1 - zh)
 
         for half_at, ready in enumerate(SCATTER_READY):
             first = (x // 2 + 1 + half_at) % 2
             at = pl.ds(pl.multiple_of(first * HALF, HALF), HALF)
-            value = (total[at, :] + product(chunk, at)).astype(jnp.bfloat16)
-            partial[pl.ds(first * 4, 4)] = value.reshape(4, OWN, VECTORS)
+            value = (total[at, :] + product(1 - zh, at)).astype(jnp.bfloat16)
+            partial[h, pl.ds(first * 4, 4)] = value.reshape(4, OWN, WIDTH)
             for n in ready:
-                p_copy(n).start()
-
-        v_copy(p, row, g_send.at[0], mate).wait_send()
-        for m in range(1, CHIPS):
-            v_copy(p, row, g_send.at[m], mate).wait_send()
-            v_copy(p, same_core[m], f_send.at[m], mate).wait_send()
-
-        arrived[p, col] = partial[col]
+                p_copy(t, n).start()
+
+        for m in GATHER_ORDER:
+            v_copy(b, row, g_send.at[h, m], mate).wait_send()
+        for m in RELAY_ORDER:
+            relay(b, m).wait_send()
+        for m in range(CHIPS):
+            share(b, m).wait_send()
+
+    def finish(t):
+        b, h = t % 4, t % 2
+        arrived[b, col] = partial[h, col]
         for j in range(1, N_COL):
             s = (col + j) % N_COL
             pltpu.make_async_remote_copy(
-                src_ref=partial.at[s],
-                dst_ref=arrived.at[p, s],
-                send_sem=p_send.at[0],
-                recv_sem=p_recv.at[p, s],
+                src_ref=partial.at[h, s],
+                dst_ref=arrived.at[b, s],
+                send_sem=p_send.at[h, 0],
+                recv_sem=p_recv.at[b, s],
                 device_id=(row, s),
                 device_id_type=MESH,
             ).wait_recv()
         for n in range(N_COL - 1):
-            p_copy(n).wait_send()
-
-        applied = arrived[p, 0].astype(jnp.float32)
+            p_copy(t, n).wait_send()
+
+        applied = arrived[b, 0].astype(jnp.float32)
         for s in range(1, N_COL):
-            applied = applied + arrived[p, s].astype(jnp.float32)
-        now = current[...]
-        scale = jnp.where(k == 0, 1.0, 2.0)
-        following = scale * (applied - center * now) / half - previous[...]
-        previous[...] = now
-        current[...] = following
-        gathered[1 - p, row // 4, pl.ds(pl.multiple_of((row % 4) * OWN, OWN), OWN), :] = (
-            following.astype(jnp.bfloat16)
-        )
+            applied = applied + arrived[b, s].astype(jnp.float32)
+        now = current[h]
+        scale = jnp.where(t < 2, 1.0, 2.0)
+        following = scale * (applied - center * now) / half - previous[h]
+        previous[h] = now
+        current[h] = following
+        return following
+
+    def turn(t, carry):
+        def finish_other():
+            @pl.when(t > 0)
+            def _():
+                following = finish(t - 1)
+
+                @pl.when(t < TURNS - 1)
+                def _():
+                    start_gather(t + 1, following.astype(jnp.bfloat16))
+
+        multiply(t, finish_other)
         return carry
 
-    lax.fori_loop(0, DEGREE, step, 0)
-    out_ref[...] = current[...]
+    lax.fori_loop(0, TURNS, turn, 0)
+    finish(TURNS - 1)
+    for h in range(2):
+        out_ref[:, h * WIDTH : (h + 1) * WIDTH] = current[h]
 
 
 def body(trial_vectors, h_blocks, block_col, block_count, center, half_width):
@@ -297,20 +341,22 @@
         out_specs=vmem,
         scratch_shapes=[
             pltpu.VMEM((PIECES, N_ROW, PIECE, BLOCK, PER * BLOCK), bf16),
-            pltpu.VMEM((CHUNKS, ROWS, CHUNK), bf16),
-            pltpu.VMEM((2, CHUNKS, CHUNK, VECTORS), bf16),
-            pltpu.VMEM((ROWS, VECTORS), f32),
-            pltpu.VMEM((N_COL, OWN, VECTORS), bf16),
-            pltpu.VMEM((2, N_COL, OWN, VECTORS), bf16),
-            pltpu.VMEM((OWN, VECTORS), f32),
-            pltpu.VMEM((OWN, VECTORS), f32),
+            pltpu.VMEM((2, ROWS, CHUNK), bf16),
+            pltpu.VMEM((4, 2, CHUNK, WIDTH), bf16),
+            pltpu.VMEM((ROWS, WIDTH), f32),
+            pltpu.VMEM((2, N_COL, OWN, WIDTH), bf16),
+            pltpu.VMEM((4, N_COL, OWN, WIDTH), bf16),
+            pltpu.VMEM((2, OWN, WIDTH), f32),
+            pltpu.VMEM((2, OWN, WIDTH), f32),
             dma((PIECES, N_ROW - 1)),
             dma((PIECES,)),
-            dma((CHIPS,)),
-            dma((CHIPS,)),
-            dma((2, N_ROW)),
-            dma((N_COL - 1,)),
-            dma((2, N_COL)),
+            dma((2, 5)),
+            dma((4,)),
+            dma((2, CHIPS)),
+            dma((4, 2)),
+            dma((4, CHIPS)),
+            dma((2, N_COL - 1)),
+            dma((4, N_COL)),
         ],
         compiler_params=pltpu.CompilerParams(
             collective_id=0, has_side_effects=True, vmem_limit_bytes=48 * 2**20

time: 250 us -> 216 us (0.86)
  Pallas kernels: 245 us -> 211 us
    pallas_call x1, Pallas kernels: 245 us -> 211 us  [body(): pl.pallas_call(kernel, out_shape=jax.ShapeDtypeStruct((OWN, VECTORS), f32...]
where the time goes in v3:
time: 216 us
  Pallas kernels  211 us (98%)
  local copies, waits for them, and re-layouts  2.24 us (1%)
    pallas_call x1, Pallas kernels, body(): pl.pallas_call(kernel, out_shape=jax.ShapeDtypeStruct((OWN, VECTORS), f32...  211 us

profile of v3, /device:TPU:1, one launch (start us, length us, event | category | flops | bytes accessed | tf_op | source)
XLA Modules:
  0.0 216.0 jit_solution(14735965278246074645)
XLA Ops:
  0.0 0.7 compare_select_fusion
  0.7 0.2 copy.8
  0.9 0.6 compare_convert_fusion
  1.5 0.5 reshape.16.coef_ref
  3.3 0.1 pad_maximum_fusion.scal_ref
  3.4 0.0 copy-start
  3.4 0.9 copy-done
  4.3 211.0 %filter.1 = f32[192,256]{1,0:T(8,128)S(1)} custom-call(f32[2304]{0:T(1024)S(1)} %reshape.16.coef_ref, f32[2]{0:T(128)S(1)} %pad_maximum_fusion.scal_ref, bf16[192,256]{1,0:T(8,128)(2,1)S(1)} %copy-done, bf16[16,24,64,128]{3,2,1,0:T(8,128)(2,1)} %bitcast.4), custom_call_target="tpu_custom_call" | custom-call | tf_op jit(solution)/shard_map/filter/pallas_call | solution.py:337
  215.3 0.7 copy.12
Async XLA Ops:
  3.4 0.9 copy-start

commit v4 on v3

--- a/solution.py
+++ b/solution.py
@@ -19,7 +19,7 @@
 ROWS = DOMAIN * BLOCK
 CHIPS = 8
 CHUNK = 8 * OWN
-PIECES = 8
+PIECES = 12
 PIECE = DOMAIN // PIECES
 MESH = pl.DeviceIdType.MESH
 GATHER_ORDER = (4, 1, 3, 2)
@@ -39,11 +39,14 @@
 
 
 def kernel(
-    coef_ref,
-    scal_ref,
-    trial_ref,
+    code_ref,
+    center_ref,
+    half_ref,
+    trial_in,
     h_ref,
     out_ref,
+    trial_ref,
+    trial_sem,
     hbuf,
     dense,
     gathered,
@@ -78,6 +81,8 @@
         (zh if m < 4 else 1 - zh) * 8 + pair_y(m % 4) * 2 + core for m in range(CHIPS)
     ]
 
+    trial_copy = pltpu.make_async_copy(trial_in, trial_ref, trial_sem)
+    trial_copy.start()
     barrier = pltpu.get_barrier_semaphore()
     for step_to in H_ORDER:
         pl.semaphore_signal(
@@ -88,6 +93,7 @@
             barrier, inc=1, device_id=(row, (col + j) % N_COL), device_id_type=MESH
         )
     pl.semaphore_wait(barrier, N_ROW + N_COL - 2)
+    trial_copy.wait()
 
     def v_rows(s):
         place = (s % 2) * 4 + (s // 2) % 4
@@ -170,7 +176,7 @@
             i = piece * PIECE + at_piece
 
             def coef(s, q, j):
-                return coef_ref[((i * N_ROW + s) * PER + q) * BLOCK_ROWS + j]
+                return jnp.where(code_ref[(i * N_ROW + s) * PER + q] == j, 1.0, 0.0)
 
             def lanes(a, b):
                 return jnp.where(left, a, b)
@@ -220,7 +226,7 @@
 
     lax.fori_loop(0, PIECES, h_sent, 0)
 
-    center, half = scal_ref[0], scal_ref[1]
+    center, half = center_ref[0], half_ref[0]
     HALF = ROWS // 2
 
     def p_copy(t, n):
@@ -326,20 +332,19 @@
     slot = lax.broadcasted_iota(jnp.int32, (DOMAIN, N_ROW, PER), 2)
     filled = slot < block_count[0, 0][:, :, None]
     code = jnp.where(filled, block_col[0, 0], -1)
-    coef = (code[..., None] == jnp.arange(BLOCK_ROWS, dtype=jnp.int32)).astype(jnp.float32)
-    scal = jnp.concatenate([center, half_width])
-    vmem, smem = (
-        pl.BlockSpec(memory_space=pltpu.VMEM),
-        pl.BlockSpec(memory_space=pltpu.SMEM),
+    vmem, smem, hbm = (
+        pl.BlockSpec(memory_space=space) for space in (pltpu.VMEM, pltpu.SMEM, pl.ANY)
     )
     dma = pltpu.SemaphoreType.DMA
     bf16, f32 = jnp.bfloat16, jnp.float32
     return pl.pallas_call(
         kernel,
         out_shape=jax.ShapeDtypeStruct((OWN, VECTORS), f32),
-        in_specs=[smem, smem, vmem, pl.BlockSpec(memory_space=pl.ANY)],
+        in_specs=[smem, smem, smem, hbm, hbm],
         out_specs=vmem,
         scratch_shapes=[
+            pltpu.VMEM((OWN, VECTORS), bf16),
+            dma,
             pltpu.VMEM((PIECES, N_ROW, PIECE, BLOCK, PER * BLOCK), bf16),
             pltpu.VMEM((2, ROWS, CHUNK), bf16),
             pltpu.VMEM((4, 2, CHUNK, WIDTH), bf16),
@@ -362,7 +367,7 @@
             collective_id=0, has_side_effects=True, vmem_limit_bytes=48 * 2**20
         ),
         name="filter",
-    )(coef.reshape(-1), scal, trial_vectors, h_blocks[0, :, :, :, 0, :])
+    )(code.reshape(-1), center, half_width, trial_vectors, h_blocks[0, :, :, :, 0, :])
 
 
 def solution(mesh):

time: 216 us -> 215 us (level)
  no operation moved by 1% of the time
where the time goes in v4:
time: 215 us
  Pallas kernels  210 us (98%)
  local copies, waits for them, and re-layouts  3.53 us (2%)
    pallas_call x1, Pallas kernels, body(): pl.pallas_call(kernel, out_shape=jax.ShapeDtypeStruct((OWN, VECTORS), f32...  210 us

profile of v4, /device:TPU:1, one launch (start us, length us, event | category | flops | bytes accessed | tf_op | source)
XLA Modules:
  0.0 215.1 jit_solution(6082752985992864270)
XLA Ops:
  1.3 0.8 copy.8
  2.1 0.1 iota_compare_fusion
  2.2 0.2 lt.17
  2.4 0.9 copy.9
  3.3 0.1 squeeze.6
  3.4 0.0 copy-start
  3.4 0.9 copy-done
  4.3 210.1 %filter.1 = f32[192,256]{1,0:T(8,128)S(1)} custom-call(s32[768]{0:T(1024)S(1)} %broadcast_select_fusion.code_ref, f32[1]{0:T(128)S(6)} %copy.11.center_ref, f32[1]{0:T(128)S(6)} %copy.12.half_ref, bf16[192,256]{1,0:T(8,128)(2,1)S(1)} %copy-done, bf16[16,24,64,128]{3,2,1,0:T(8,128)(2,1)} %bitcast.4), custom_call_target="tpu_custom_call" | custom-call | tf_op jit(solution)/shard_map/filter/pallas_call | solution.py:340
  214.4 0.7 copy.13
  (1 shorter events, 0.0 us)
Async XLA Ops:
  3.4 0.9 copy-start

commit v5 on v4

--- a/solution.py
+++ b/solution.py
@@ -259,6 +259,14 @@
                     relay(b, n).start()
             share(b, m).start()
 
+        def core_product(of_core, rows_at):
+            k = pl.ds(pl.multiple_of(of_core * (CHUNK // 2), CHUNK // 2), CHUNK // 2)
+            return jnp.dot(
+                dense[1 - zh, rows_at, k],
+                gathered[b, 1 - zh, k, :],
+                preferred_element_type=jnp.float32,
+            )
+
         for m in ARRIVAL_ORDER[:FINISH_AT]:
             arrive(m)
         shared(b, zh)
@@ -266,12 +274,13 @@
         finish_other()
         for m in ARRIVAL_ORDER[FINISH_AT:]:
             arrive(m)
+        total[...] += core_product(core, slice(None))
         shared(b, 1 - zh)
 
         for half_at, ready in enumerate(SCATTER_READY):
             first = (x // 2 + 1 + half_at) % 2
             at = pl.ds(pl.multiple_of(first * HALF, HALF), HALF)
-            value = (total[at, :] + product(1 - zh, at)).astype(jnp.bfloat16)
+            value = (total[at, :] + core_product(1 - core, at)).astype(jnp.bfloat16)
             partial[h, pl.ds(first * 4, 4)] = value.reshape(4, OWN, WIDTH)
             for n in ready:
                 p_copy(t, n).start()
@@ -296,9 +305,6 @@
                 device_id=(row, s),
                 device_id_type=MESH,
             ).wait_recv()
-        for n in range(N_COL - 1):
-            p_copy(t, n).wait_send()
-
         applied = arrived[b, 0].astype(jnp.float32)
         for s in range(1, N_COL):
             applied = applied + arrived[b, s].astype(jnp.float32)
@@ -309,6 +315,10 @@
         current[h] = following
         return following
 
+    def scattered(t):
+        for n in range(N_COL - 1):
+            p_copy(t, n).wait_send()
+
     def turn(t, carry):
         def finish_other():
             @pl.when(t > 0)
@@ -319,11 +329,14 @@
                 def _():
                     start_gather(t + 1, following.astype(jnp.bfloat16))
 
+                scattered(t - 1)
+
         multiply(t, finish_other)
         return carry
 
     lax.fori_loop(0, TURNS, turn, 0)
     finish(TURNS - 1)
+    scattered(TURNS - 1)
     for h in range(2):
         out_ref[:, h * WIDTH : (h + 1) * WIDTH] = current[h]
 

time: 215 us -> 208 us (0.967)
  Pallas kernels: 210 us -> 203 us
    pallas_call x1, Pallas kernels: 210 us -> 203 us  [body(): pl.pallas_call(kernel, out_shape=jax.ShapeDtypeStruct((OWN, VECTORS), f32...]
where the time goes in v5:
time: 208 us
  Pallas kernels  203 us (98%)
  local copies, waits for them, and re-layouts  3.53 us (2%)
    pallas_call x1, Pallas kernels, body(): pl.pallas_call(kernel, out_shape=jax.ShapeDtypeStruct((OWN, VECTORS), f32...  203 us

profile of v5, /device:TPU:1, one launch (start us, length us, event | category | flops | bytes accessed | tf_op | source)
XLA Modules:
  0.0 207.8 jit_solution(12087484707408418015)
XLA Ops:
  1.3 0.8 copy.8
  2.1 0.1 iota_compare_fusion
  2.2 0.2 lt.17
  2.4 0.9 copy.9
  3.3 0.1 squeeze.6
  3.4 0.0 copy-start
  3.4 0.9 copy-done
  4.3 202.8 %filter.1 = f32[192,256]{1,0:T(8,128)S(1)} custom-call(s32[768]{0:T(1024)S(1)} %broadcast_select_fusion.code_ref, f32[1]{0:T(128)S(6)} %copy.11.center_ref, f32[1]{0:T(128)S(6)} %copy.12.half_ref, bf16[192,256]{1,0:T(8,128)(2,1)S(1)} %copy-done, bf16[16,24,64,128]{3,2,1,0:T(8,128)(2,1)} %bitcast.4), custom_call_target="tpu_custom_call" | custom-call | tf_op jit(solution)/shard_map/filter/pallas_call | solution.py:353
  207.2 0.7 copy.13
  (1 shorter events, 0.0 us)
Async XLA Ops:
  3.4 0.9 copy-start
